TPU v7x, 32 devices: a whole 2x2x4 slice. The times are simulated.
32 devices in a mesh: wa: 2 (over x), uv: 16 (over z, y, core).
Axes of the slice: x: 2, y: 2, z: 4, core: 2. Of those that a mesh axis runs over, the one named last changes fastest.
Arguments:
- visibility: bfloat16 [1536, 2, 256], P(('wa', 'uv')), may hold values from -6 to 6
- coords: bfloat16 [1536, 2, 256], P(('wa', 'uv')), may hold values from -24 to 24
- tile_row: int32 [1536, 1], P(('wa', 'uv')), may hold values from 0 to 63; in each aligned block of 48 rows (0 to 47, 48 to 95, ...) at most 2 rows name the same one
- col_offset: int32 [1536], P(('wa', 'uv')), may hold values from 0 to 4032
- live_count: int32 [2, 16], P('wa', 'uv'), may hold values from 1 to 48, 480 in all within a row
Outputs:
- sky_image: float32 [4096, 4096], P('uv', 'wa')
Inputs may be any that keep to these rules, and one draw needn't show every extreme that they name: `tile_row`: within the blocks of one device, at most 2 name the same tile row, and some device reaches 2. A device's live blocks are its first live_count ones; in each w group the 16 counts sum to 480, and the largest count is 48.
All inputs are finite; a program needn't handle non-finite values.
Results may differ from a plain program's by a relative error of at most 0.0069.
Values may be sent and summed in bfloat16 or wider, within the bound.
A program may use at most 128 MiB of HBM per device.

v0:
```python
import functools
import math

import jax
import jax.numpy as jnp
import ml_dtypes
import numpy as np
from jax import lax
from jax.experimental import pallas as pl
from jax.experimental.pallas import tpu as pltpu
from jax.sharding import PartitionSpec as P

G = 4096
SUB = 64
UNROLL = 4
plane_step = 6.0
full_turn = 2.0 * math.pi
BF = ml_dtypes.bfloat16


def turn_poly():
    nodes = np.cos(np.pi * (np.arange(256) + 0.5) / 256)
    z = (nodes + 1.0) / 8.0
    f = np.sqrt(z)
    cos_c = np.polynomial.chebyshev.cheb2poly(
        np.polynomial.chebyshev.chebfit(nodes, np.cos(2 * np.pi * f), 7)
    )
    sin_c = np.polynomial.chebyshev.cheb2poly(
        np.polynomial.chebyshev.chebfit(nodes, np.sin(2 * np.pi * f) / f, 7)
    )
    base = np.polynomial.Polynomial([-1.0, 8.0])
    out = []
    for coefs in (cos_c, sin_c):
        total = np.polynomial.Polynomial([0.0])
        for c in coefs[::-1]:
            total = total * base + c
        out.append([float(c) for c in total.coef])
    return out


COS_C, SIN_C = turn_poly()


def cos_sin_turns(turns):
    f = turns - jnp.round(turns)
    z = f * f
    c = jnp.full_like(z, COS_C[-1])
    for k in COS_C[-2::-1]:
        c = c * z + k
    s = jnp.full_like(z, SIN_C[-1])
    for k in SIN_C[-2::-1]:
        s = s * z + k
    return c, s * f


def factor_table():
    o = np.arange(SUB) - SUB // 2
    ang = full_turn / SUB * np.mod(o[:, None] * o[None, :], SUB)
    return np.cos(ang).astype(BF), (-np.sin(ang)).astype(BF)


def factor_matrix():
    fr, fi = factor_table()
    return np.block([[fr, -fi], [fi, fr]]).astype(BF)


def head_matrix():
    k = np.arange(64)
    ang = full_turn / 64 * np.mod(k[:, None] * k[None, :], 64)
    c, s = np.cos(ang), np.sin(ang)
    return np.block([[c, -s], [s, c]]).astype(BF)


def tail_matrices():
    l0 = np.arange(64)[:, None, None]
    p = np.arange(64)[None, :, None]
    l1 = np.arange(64)[None, None, :]
    ang = full_turn / G * np.mod(p * (l0 + 64 * l1), G)
    sign = 1.0 - 2.0 * ((p + l0) % 2)
    c, s = np.cos(ang) * sign, np.sin(ang) * sign
    top = np.concatenate([c, s], axis=2)
    bottom = np.concatenate([-s, c], axis=2)
    return np.concatenate([top, bottom], axis=1).astype(BF)


def grid_kernel(width, tiles, counts, data_ref, phase_ref, mf_ref, d_ref, out_ref, acc):
    j = pl.program_id(0)
    blocks = data_ref.shape[0]

    @pl.when(j == 0)
    def _():
        acc[...] = jnp.zeros_like(acc)

    total = counts[j]
    offs = lax.broadcasted_iota(jnp.int32, (8, data_ref.shape[2]), 0).astype(jnp.float32)
    fine = offs * (1.0 / SUB)
    coarse = (offs - 4.0) * (8.0 / SUB)
    scale = 1.0 / math.sqrt(data_ref.shape[2])

    def expand(pr, pi, c1, s1):
        res, ims = [], []
        for a in range(8):
            ar, ai = pr[a : a + 1, :], pi[a : a + 1, :]
            res.append(ar * c1 - ai * s1)
            ims.append(ar * s1 + ai * c1)
        return jnp.concatenate(res + ims, axis=0).astype(jnp.bfloat16)

    def step(it, carry):
        lefts, rights = [], []
        for k in range(UNROLL):
            i = it * UNROLL + k
            keep = jnp.where(i < total, scale, 0.0)
            row = data_ref[i]
            vr, vi, u, v = (row[n : n + 1, :] for n in range(4))
            c1, s1 = cos_sin_turns(fine * u)
            c8, s8 = cos_sin_turns(coarse * u)
            lefts.append(
                expand((vr * c8 - vi * s8) * keep, (vr * s8 + vi * c8) * keep, c1, s1)
            )
            d1, t1 = cos_sin_turns(fine * v)
            d8, t8 = cos_sin_turns(coarse * v)
            rights.append(expand(d8, t8, d1, t1))
        parts = []
        for k in range(UNROLL):
            s = lax.dot_general(
                lefts[k], rights[k], (((1,), (1,)), ((), ())), preferred_element_type=jnp.float32
            ).astype(jnp.bfloat16)
            c = jnp.dot(mf_ref[...], s, preferred_element_type=jnp.float32).astype(jnp.bfloat16)
            parts.append(jnp.concatenate([c[:SUB], c[SUB:]], axis=1))
        h = jnp.dot(jnp.concatenate(parts, axis=0), d_ref[...], preferred_element_type=jnp.float32)
        for k in range(UNROLL):
            i = it * UNROLL + k
            ph = phase_ref[i]
            pr, pi = ph[0:1, :], ph[1:2, :]
            hr = h[k * SUB : (k + 1) * SUB, :width]
            hi = h[k * SUB : (k + 1) * SUB, width:]
            rows = pl.ds(pl.multiple_of(tiles[j * blocks + i] * SUB, SUB), SUB)
            acc[0, rows, :] += hr * pr - hi * pi
            acc[1, rows, :] += hr * pi + hi * pr
        return carry

    lax.fori_loop(0, (total + UNROLL - 1) // UNROLL, step, 0)

    @pl.when(j == pl.num_programs(0) - 1)
    def _():
        out_ref[...] = acc[...].astype(jnp.bfloat16)


def on_device(visibility, coords, tile_row, col_offset, live_count):
    uv_count = lax.axis_size("uv")
    wa_count = lax.axis_size("wa")
    uv_index = lax.axis_index("uv")
    wa_index = lax.axis_index("wa")
    blocks = visibility.shape[0]
    k_len = visibility.shape[2]
    width = G // uv_count
    placement = jnp.concatenate(
        [tile_row[:, 0], col_offset, jnp.broadcast_to(live_count[0], (blocks,))]
    )
    all_place = lax.all_gather(placement, "uv", axis=0).reshape(uv_count, 3, blocks)
    tiles = all_place[:, 0].reshape(-1)
    cols = all_place[:, 1].reshape(-1)
    counts = all_place[:, 2, 0]
    data = jnp.concatenate([visibility, coords], axis=1)
    all_data = lax.all_gather(data, "uv", axis=0, tiled=True).astype(jnp.float32)

    m_off = uv_index * width + jnp.arange(width) - G // 2
    turn = jnp.mod((cols[:, None] - G // 2) * m_off[None, :], G).astype(jnp.float32) * (1.0 / G)
    pc, ps = cos_sin_turns(turn)
    phase = jnp.stack([pc, ps], axis=1)

    fr, fi = factor_table()
    fr, fi = jnp.asarray(fr.astype(np.float32)), jnp.asarray(fi.astype(np.float32))
    qt = jnp.mod(jnp.arange(SUB)[:, None] * m_off[None, :], G).astype(jnp.float32) * (1.0 / G)
    qc, qs = cos_sin_turns(qt)
    mm = functools.partial(jnp.einsum, "qk,qm->km", precision=lax.Precision.HIGHEST)
    dr = (mm(fr, qc) - mm(fi, qs)) * (1.0 / SUB)
    di = (mm(fr, qs) + mm(fi, qc)) * (1.0 / SUB)
    ddr = jnp.concatenate([dr, -di], axis=0)
    ddi = jnp.concatenate([di, dr], axis=0)
    d_table = jnp.concatenate(
        [jnp.concatenate([ddr, ddi], axis=1), jnp.concatenate([-ddi, ddr], axis=1)], axis=0
    ).astype(jnp.bfloat16)

    spec = pltpu.PrefetchScalarGridSpec(
        num_scalar_prefetch=2,
        grid=(uv_count,),
        in_specs=[
            pl.BlockSpec((blocks, 4, k_len), lambda j, *_: (j, 0, 0)),
            pl.BlockSpec((blocks, 2, width), lambda j, *_: (j, 0, 0)),
            pl.BlockSpec((2 * SUB, 2 * SUB), lambda j, *_: (0, 0)),
            pl.BlockSpec((4 * SUB, 2 * width), lambda j, *_: (0, 0)),
        ],
        out_specs=pl.BlockSpec((2, G, width), lambda j, *_: (0, 0, 0)),
        scratch_shapes=[pltpu.VMEM((2, G, width), jnp.float32)],
    )
    half = pl.pallas_call(
        functools.partial(grid_kernel, width),
        out_shape=jax.ShapeDtypeStruct((2, G, width), jnp.bfloat16),
        grid_spec=spec,
        compiler_params=pltpu.CompilerParams(vmem_limit_bytes=40 * 1024 * 1024),
    )(tiles, counts, all_data, phase, jnp.asarray(factor_matrix()), d_table)

    first = jnp.dot(
        jnp.asarray(head_matrix()),
        half.reshape(2 * 64, 64 * width),
        preferred_element_type=jnp.float32,
    ).astype(jnp.bfloat16)
    first = first.reshape(2, 64, 64, width).transpose(1, 0, 2, 3).reshape(64, 128, width)
    image = jnp.einsum(
        "lxm,lxy->lmy", first, jnp.asarray(tail_matrices()), preferred_element_type=jnp.float32
    )
    l_of = jnp.arange(64)[:, None, None] + 64 * jnp.arange(64)[None, None, :] - G // 2
    x = l_of.astype(jnp.float32) / G
    y = m_off[None, :, None].astype(jnp.float32) / G
    depth_term = jnp.sqrt(1.0 - y**2 - x**2)
    depth = (wa_index.astype(jnp.float32) - (wa_count - 1) / 2.0) * plane_step
    sc, ss = cos_sin_turns(depth * (depth_term - 1.0))
    screened = (image[:, :, :64] * sc - image[:, :, 64:] * ss) * (1.0 / G)
    share = 64 // wa_count
    if wa_count == 2:
        there = lax.dynamic_slice_in_dim(screened, (1 - wa_index) * share, share, 2)
        here = lax.dynamic_slice_in_dim(screened, wa_index * share, share, 2)
        came = lax.ppermute(
            there.transpose(1, 2, 0).reshape(width, -1).astype(jnp.bfloat16),
            "wa",
            [(0, 1), (1, 0)],
        )
        return here.transpose(1, 2, 0).reshape(width, -1) + came.astype(jnp.float32)
    parts = screened.transpose(1, 2, 0).reshape(width, G).astype(jnp.bfloat16)
    parts = parts.reshape(width, wa_count, G // wa_count)
    came = lax.all_to_all(parts, "wa", split_axis=1, concat_axis=1)
    return jnp.sum(came.astype(jnp.float32), axis=1)


def solution(mesh):
    in_specs = (
        P(("wa", "uv"), None, None),
        P(("wa", "uv"), None, None),
        P(("wa", "uv"), None),
        P(("wa", "uv")),
        P("wa", "uv"),
    )
    return jax.shard_map(
        on_device, mesh=mesh, in_specs=in_specs, out_specs=P("uv", "wa"), check_vma=False
    )
```

profile of v0, /device:TPU:0, one launch (start us, length us, event | category | flops | bytes accessed | tf_op | source)
XLA Modules:
  0.0 274.3 jit_solution(17996178665608432175)
XLA Ops:
  6.5 0.0 all-gather.3.cloned.1.call-start
  6.5 1.6 pad_maximum_fusion.2
  8.1 0.0 all-gather.3.cloned.1.call-update
  8.8 1.3 dynamic-slice
  10.8 0.9 add_dynamic-update-slice_fusion
  11.7 63.2 %all-reduce = s32[2304]{0:T(1024)S(1)} all-reduce(s32[2304]{0:T(1024)S(1)} %add_dynamic-update-slice_fusion), channel_id=2, replica_groups=mesh['wa'=2,'uv'=16] {'uv'}, use_global_device_ids=true, to_apply=%add | all-reduce | flops 2304 | bytes 18432
  74.8 0.1 reshape.290
  74.9 0.1 fusion.37
  75.0 0.1 sub.75
  75.0 0.1 reshape_squeeze.3.tiles
  75.1 1.0 fusion.34
  76.2 1.0 fusion.14
  77.2 1.0 fusion.36
  78.3 1.0 fusion.86
  79.3 0.4 slice_reduce_fusion.counts
  79.8 0.4 fusion.16
  80.2 7.2 %multiply_add_fusion = (f32[768,1,256]{2,1,0:T(1,128)S(1)}, f32[768,1,256]{2,1,0:T(1,128)S(1)}) fusion(f32[768,1,256]{2,0,1:T(8,128)S(1)} %fusion.16), kind=kLoop, calls=%fused_computation.45 | loop fusion | flops 6488064 | bytes 2359296 | tf_op jit(solution)/shard_map/add | solution.py:49
  87.4 0.0 copy-start.1
  87.4 1.4 pad_maximum_fusion.phase_ref
  88.9 0.0 all-gather.3.cloned.1.call-done
  88.9 1.8 convert_element_type.58.data_ref
  90.7 0.0 copy-done.1
  90.7 116.6 %shard_map.100 = bf16[2,4096,256]{2,1,0:T(8,128)(2,1)S(1)} custom-call(s32[768]{0:T(1024)S(1)} %reshape_squeeze.3.tiles, s32[16]{0:T(128)S(1)} %slice_reduce_fusion.counts, f32[768,4,256]{2,1,0:T(4,128)S(1)} %convert_element_type.58.data_ref, f32[768,2,256]{2,1,0:T(2,128)S(1)} %pad_maximum_fusion.phase_ref, bf16[128,128]{1,0:T(8,128)(2,1)S(1)} %copy-done.1, ...), custom_call_target="tpu_custom_call" | custom-call | tf_op jit(solution)/shard_map/pallas_call | solution.py:197
  207.3 0.0 copy-start
  207.3 2.0 copy-done
  209.3 0.0 copy-start.4
  209.3 7.4 %reshape.291 = bf16[128,16384]{1,0:T(8,128)(2,1)} reshape(bf16[2,4096,256]{2,1,0:T(8,128)(2,1)} %copy-done) | data formatting | bytes 8388608 | tf_op jit(solution)/shard_map/reshape | solution.py:206
  216.7 0.0 copy-done.4
  216.7 5.4 %fusion = bf16[128,16384]{0,1:T(8,128)(2,1)} fusion(bf16[128,16384]{1,0:T(8,128)(2,1)} %reshape.291, bf16[128,128]{1,0:T(8,128)(2,1)S(1)} %copy-done.4), kind=kOutput, calls=%fused_computation.1 | convolution fusion | flops 538968064 | bytes 8421376 | tf_op jit(solution)/shard_map/dot_general | solution.py:204
  222.1 6.4 %copy.27 = bf16[128,16384]{1,0:T(8,128)(2,1)} copy(bf16[128,16384]{0,1:T(8,128)(2,1)} %fusion) | data formatting | bytes 8388608 | tf_op jit(solution)/shard_map/convert_element_type | solution.py:208
  228.5 3.4 %copy.32 = bf16[16,8,64,256]{3,2,1,0:T(8,128)(2,1)S(1)} copy(bf16[16,8,64,256]{3,1,2,0:T(8,128)(2,1)} %bitcast.34) | data formatting | bytes 8388608
  231.9 0.6 bitcast_bitcast_fusion
  232.5 0.0 copy-start.3
  232.5 0.6 copy.28
  233.1 1.0 copy-done.3
  234.1 1.2 fusion.87
  235.3 6.7 %fusion.2 = f32[64,256,64]{1,2,0:T(8,128)S(1)} fusion(f32[64,256,128]{1,2,0:T(8,128)S(1)} %fusion.87, f32[64,64]{1,0:T(8,128)S(1)} %multiply_multiply_fusion.16, f32[256]{0:T(256)S(1)} %multiply_subtract_fusion, f32[]{:T(128)S(6)} %mul.384), kind=kLoop, calls=%fused_computation.6 | loop fusion | flops 40894464 | bytes 12600324 | tf_op jit(solution)/shard_map/mul | solution.py:219
  242.1 0.0 copy-start.2
  242.1 1.9 copy-done.2
  244.0 0.2 fusion.15
  244.2 0.6 copy.30
  244.7 0.6 collective-permute-start
  245.3 1.8 dynamic-slice_bitcast_fusion
  247.2 1.2 copy.29
  248.4 17.0 %collective-permute-done = bf16[256,2048]{0,1:T(8,128)(2,1)S(1)} collective-permute-done((bf16[256,2048]{0,1:T(8,128)(2,1)S(1)}, bf16[256,2048]{0,1:T(8,128)(2,1)S(1)}, u32[]{:S(2)}, u32[]{:S(2)}) %collective-permute-start) | collective-permute-done | bytes 1048608 | tf_op jit(solution)/shard_map/ppermute | solution.py:224
  265.4 0.2 bitcast_add_fusion
  265.6 1.8 copy.31
  (9 shorter events, 0.1 us)
Async XLA Ops:
  6.5 82.4 %all-gather.3.cloned.1.call-start = ((), (), s32[]{:S(2)}) async-start(), calls=%async_computation | async-start | bytes 1671168 | tf_op jit(solution)/shard_map/all_gather | solution.py:165
  87.4 3.3 %copy-start.1 = (bf16[128,128]{1,0:T(8,128)(2,1)S(1)}, bf16[128,128]{1,0:T(8,128)(2,1)}, u32[]{:S(2)}) copy-start(bf16[128,128]{1,0:T(8,128)(2,1)} %constant.71.clone.mf_ref) | copy-start | bytes 98308
  207.3 2.0 copy-start
  209.3 7.4 %copy-start.4 = (bf16[128,128]{1,0:T(8,128)(2,1)S(1)}, bf16[128,128]{1,0:T(8,128)(2,1)}, u32[]{:S(2)}) copy-start(bf16[128,128]{1,0:T(8,128)(2,1)} %constant.72.clone) | copy-start | bytes 98308
  232.5 1.6 copy-start.3
  242.1 1.9 copy-start.2
  244.7 20.6 %collective-permute-start = (bf16[256,2048]{0,1:T(8,128)(2,1)S(1)}, bf16[256,2048]{0,1:T(8,128)(2,1)S(1)}, u32[]{:S(2)}, u32[]{:S(2)}) collective-permute-start(bf16[256,2048]{0,1:T(8,128)(2,1)S(1)} %bitcast.36), channel_id=1, source_target_pairs={{0,16},{16,0},{1,17},{17,1},{2,18},{18,2},{3,19},{19,3},{4,20},{20... | collective-permute-start | bytes 3145736 | tf_op jit(solution)/shard_map/ppermute | solution.py:224
Sparse Core Ops, SparseCore 0:
  9.6 42.4 all-gather.2
where the time goes:
time: 275 us; the launch traced here: 274 us
  Pallas kernels  117 us (43%)
  blocking collectives  63.2 us (23%)
  local copies, waits for them, and re-layouts  30.7 us (11%)
  other arithmetic  20.4 us (7%)
  waiting for transfers between devices  17 us (6%)
  between operations  15 us (5%)
  matrix products  10.8 us (4%)
    pallas_call x1, Pallas kernels, on_device(): pl.pallas_call(functools.partial(grid_kernel, width), out_shape=jax.Shape...  117 us
    unnamed x1, blocking collectives  63.2 us
    ppermute x1, waiting for transfers between devices, on_device(): lax.ppermute(there.transpose(1, 2, 0).reshape(width, -1).astype(jnp.bfloa...  17 us
    unnamed x13, local copies, waits for them, and re-layouts  9.61 us
    reshape x1, local copies, waits for them, and re-layouts, on_device(): half.reshape(2 * 64, 64 * width)  7.39 us
    add x1, other arithmetic, cos_sin_turns(): c = c * z + k  7.25 us
    mul x1, other arithmetic, on_device(): screened = (image[:, :, :64] * sc - image[:, :, 64:] * ss) * (1.0 / G)  6.74 us
    convert_element_type x1, local copies, waits for them, and re-layouts, on_device(): first = jnp.dot(jnp.asarray(head_matrix()), half.reshape(2 * 64, 64 * wid...  6.36 us
  transfers between devices with their start and end apart: 2, of which 1 were waited for; matrix products, arithmetic and copies ran while one was open for 7% of the time, Pallas kernels for 0%

commit v1 on v0

--- a/solution.py
+++ b/solution.py
@@ -64,11 +64,18 @@
     return np.block([[fr, -fi], [fi, fr]]).astype(BF)
 
 
-def head_matrix():
-    k = np.arange(64)
-    ang = full_turn / 64 * np.mod(k[:, None] * k[None, :], 64)
-    c, s = np.cos(ang), np.sin(ang)
-    return np.block([[c, -s], [s, c]]).astype(BF)
+def head_matrices():
+    l0 = np.arange(64)[:, None]
+    out = []
+    for core in range(2):
+        columns = []
+        for source in range(2):
+            t = (2 * np.arange(32) + (core ^ source))[None, :]
+            ang = full_turn / 64 * np.mod(l0 * t, 64)
+            c, s = np.cos(ang), np.sin(ang)
+            columns.append(np.block([[c, -s], [s, c]]))
+        out.append(np.concatenate(columns, axis=1))
+    return np.stack(out).astype(BF)
 
 
 def tail_matrices():
@@ -83,19 +90,117 @@
     return np.concatenate([top, bottom], axis=1).astype(BF)
 
 
-def grid_kernel(width, tiles, counts, data_ref, phase_ref, mf_ref, d_ref, out_ref, acc):
+def gather_kernel(far, near, x_ref, out_ref, z_send, z_recv, y_send, y_recv, c_send, c_recv):
+    me = lax.axis_index("uv")
+    c = lax.rem(me, 2)
+    b = lax.rem(me // 2, near)
+    a = me // (2 * near)
+
+    def at(da, db, dc):
+        return (
+            lax.rem(a + da + far, far) * near + lax.rem(b + db + near, near)
+        ) * 2 + lax.rem(c + dc, 2)
+
+    peers = [at(d, 0, 0) for d in range(1, far)]
+    peers += [at(0, e, 0) for e in range(1, near)] + [at(0, 0, 1)]
+    barrier = pltpu.get_barrier_semaphore()
+    for peer in peers:
+        pl.semaphore_signal(
+            barrier, inc=1, device_id={"uv": peer}, device_id_type=pl.DeviceIdType.MESH
+        )
+    pl.semaphore_wait(barrier, len(peers))
+
+    def copy(source, slot, target, send, recv):
+        return pltpu.make_async_remote_copy(
+            src_ref=source,
+            dst_ref=out_ref.at[slot],
+            send_sem=send,
+            recv_sem=recv,
+            device_id={"uv": target},
+            device_id_type=pl.DeviceIdType.MESH,
+        )
+
+    sent = []
+
+    def send(source, slot, target, send_sem, recv_sem):
+        one = copy(source, slot, target, send_sem, recv_sem)
+        one.start()
+        sent.append(one)
+
+    for d in range(1, far):
+        send(x_ref, me, at(d, 0, 0), z_send.at[d], z_recv.at[d])
+    for d in range(far):
+        slot = at(-d, 0, 0)
+        source = x_ref if d == 0 else out_ref.at[slot]
+        if d > 0:
+            copy(x_ref, slot, me, z_send.at[d], z_recv.at[d]).wait_recv()
+        for e in range(1, near):
+            k = d * near + e
+            send(source, slot, at(0, e, 0), y_send.at[k], y_recv.at[k])
+        k = d * near
+        send(source, slot, at(0, 0, 1), c_send.at[k], c_recv.at[k])
+        if d == 0:
+            out_ref[me] = x_ref[...]
+    for d in range(far):
+        for e in range(1, near):
+            k = d * near + e
+            slot = at(-d, -e, 0)
+            copy(x_ref, slot, me, y_send.at[k], y_recv.at[k]).wait_recv()
+            send(out_ref.at[slot], slot, at(0, 0, 1), c_send.at[k], c_recv.at[k])
+    for d in range(far):
+        for e in range(near):
+            k = d * near + e
+            copy(x_ref, at(-d, -e, 1), me, c_send.at[k], c_recv.at[k]).wait_recv()
+    for one in sent:
+        one.wait_send()
+
+
+def gather_all(packed, uv_count):
+    chips = uv_count // 2
+    near = 1 << ((chips.bit_length() - 1) // 2)
+    far = chips // near
+    sems = [far] * 2 + [far * near] * 4
+    return pl.pallas_call(
+        functools.partial(gather_kernel, far, near),
+        out_shape=jax.ShapeDtypeStruct((uv_count,) + packed.shape, packed.dtype),
+        in_specs=[pl.BlockSpec(memory_space=pltpu.VMEM)],
+        out_specs=pl.BlockSpec(memory_space=pltpu.VMEM),
+        scratch_shapes=[pltpu.SemaphoreType.DMA((n,)) for n in sems],
+        compiler_params=pltpu.CompilerParams(
+            collective_id=0, has_side_effects=True, vmem_limit_bytes=24 * 1024 * 1024
+        ),
+    )(packed)
+
+
+def grid_kernel(
+    width, blocks, tiles, counts, data_ref, cols_ref, moff_ref, mf_ref, d_ref,
+    keep_ref, give_ref, acc, rows_f, phase, mine,
+):
     j = pl.program_id(0)
-    blocks = data_ref.shape[0]
+    steps = pl.num_programs(0)
 
     @pl.when(j == 0)
     def _():
         acc[...] = jnp.zeros_like(acc)
 
-    total = counts[j]
-    offs = lax.broadcasted_iota(jnp.int32, (8, data_ref.shape[2]), 0).astype(jnp.float32)
+    core = counts[steps]
+    rows_f[...] = data_ref[0].astype(jnp.float32)
+    for h in range(2):
+        turn = jnp.bitwise_and((cols_ref[0] - G // 2) * moff_ref[h : h + 1, :], G - 1)
+        pc, ps = cos_sin_turns(turn.astype(jnp.float32) * (1.0 / G))
+        phase[2 * h] = pc
+        phase[2 * h + 1] = ps
+
+    def pick(i, n):
+        mine[n] = i
+        return n + jnp.where(lax.rem(tiles[j * blocks + i], 2) == core, 1, 0)
+
+    total = lax.fori_loop(0, counts[j], pick, 0)
+    k_len = data_ref.shape[2]
+    offs = lax.broadcasted_iota(jnp.int32, (8, k_len), 0).astype(jnp.float32)
     fine = offs * (1.0 / SUB)
     coarse = (offs - 4.0) * (8.0 / SUB)
-    scale = 1.0 / math.sqrt(data_ref.shape[2])
+    scale = 1.0 / math.sqrt(k_len)
 
     def expand(pr, pi, c1, s1):
         res, ims = [], []
@@ -106,12 +211,13 @@
         return jnp.concatenate(res + ims, axis=0).astype(jnp.bfloat16)
 
     def step(it, carry):
-        lefts, rights = [], []
+        lefts, rights, index = [], [], []
         for k in range(UNROLL):
-            i = it * UNROLL + k
-            keep = jnp.where(i < total, scale, 0.0)
-            row = data_ref[i]
-            vr, vi, u, v = (row[n : n + 1, :] for n in range(4))
+            n = it * UNROLL + k
+            i = jnp.where(n < total, mine[n], 0)
+            index.append(i)
+            keep = jnp.where(n < total, scale, 0.0)
+            vr, vi, u, v = (rows_f[pl.ds(q * blocks + i, 1), :] for q in range(4))
             c1, s1 = cos_sin_turns(fine * u)
             c8, s8 = cos_sin_turns(coarse * u)
             lefts.append(
@@ -127,23 +233,32 @@
             ).astype(jnp.bfloat16)
             c = jnp.dot(mf_ref[...], s, preferred_element_type=jnp.float32).astype(jnp.bfloat16)
             parts.append(jnp.concatenate([c[:SUB], c[SUB:]], axis=1))
-        h = jnp.dot(jnp.concatenate(parts, axis=0), d_ref[...], preferred_element_type=jnp.float32)
-        for k in range(UNROLL):
-            i = it * UNROLL + k
-            ph = phase_ref[i]
-            pr, pi = ph[0:1, :], ph[1:2, :]
-            hr = h[k * SUB : (k + 1) * SUB, :width]
-            hi = h[k * SUB : (k + 1) * SUB, width:]
-            rows = pl.ds(pl.multiple_of(tiles[j * blocks + i] * SUB, SUB), SUB)
-            acc[0, rows, :] += hr * pr - hi * pi
-            acc[1, rows, :] += hr * pi + hi * pr
+        joined = jnp.concatenate(parts, axis=0)
+        for h in range(2):
+            out = jnp.dot(
+                joined,
+                d_ref[:, 2 * h * width : 2 * (h + 1) * width],
+                preferred_element_type=jnp.float32,
+            )
+            for k in range(UNROLL):
+                i = index[k]
+                pr = phase[2 * h, pl.ds(i, 1), :]
+                pi = phase[2 * h + 1, pl.ds(i, 1), :]
+                hr = out[k * SUB : (k + 1) * SUB, :width]
+                hi = out[k * SUB : (k + 1) * SUB, width:]
+                rows = pl.ds(pl.multiple_of(tiles[j * blocks + i] // 2 * SUB, SUB), SUB)
+                acc[2 * h, rows, :] += hr * pr - hi * pi
+                acc[2 * h + 1, rows, :] += hr * pi + hi * pr
         return carry
 
     lax.fori_loop(0, (total + UNROLL - 1) // UNROLL, step, 0)
 
-    @pl.when(j == pl.num_programs(0) - 1)
+    @pl.when(j == steps - 1)
     def _():
-        out_ref[...] = acc[...].astype(jnp.bfloat16)
+        half_rows = acc.shape[1] // SUB
+        for h, ref in enumerate((keep_ref, give_ref)):
+            for c in range(2):
+                ref[c] = acc[2 * h + c].astype(jnp.bfloat16).reshape(half_rows, SUB, width)
 
 
 def on_device(visibility, coords, tile_row, col_offset, live_count):
@@ -154,55 +269,77 @@
     blocks = visibility.shape[0]
     k_len = visibility.shape[2]
     width = G // uv_count
-    placement = jnp.concatenate(
-        [tile_row[:, 0], col_offset, jnp.broadcast_to(live_count[0], (blocks,))]
-    )
-    all_place = lax.all_gather(placement, "uv", axis=0).reshape(uv_count, 3, blocks)
-    tiles = all_place[:, 0].reshape(-1)
-    cols = all_place[:, 1].reshape(-1)
-    counts = all_place[:, 2, 0]
-    data = jnp.concatenate([visibility, coords], axis=1)
-    all_data = lax.all_gather(data, "uv", axis=0, tiled=True).astype(jnp.float32)
+    core = jnp.mod(uv_index, 2)
+    numbers = jnp.stack(
+        [
+            tile_row[:, 0],
+            col_offset // SUB,
+            jnp.mod(col_offset, SUB),
+            jnp.broadcast_to(live_count[0], (blocks,)),
+        ]
+    )
+    numbers = jnp.pad(numbers, ((0, 12), (0, k_len - blocks))).astype(jnp.bfloat16)
+    packed = jnp.concatenate(
+        [visibility[:, 0], visibility[:, 1], coords[:, 0], coords[:, 1], numbers], axis=0
+    )
+    all_data = gather_all(packed, uv_count)
+    came_numbers = all_data[:, 4 * blocks : 4 * blocks + 4, :blocks].astype(jnp.int32)
+    tiles = came_numbers[:, 0].reshape(-1)
+    cols = (came_numbers[:, 1] * SUB + came_numbers[:, 2])[:, :, None]
+    counts = jnp.concatenate([came_numbers[:, 3, 0], core[None]])
 
     m_off = uv_index * width + jnp.arange(width) - G // 2
-    turn = jnp.mod((cols[:, None] - G // 2) * m_off[None, :], G).astype(jnp.float32) * (1.0 / G)
-    pc, ps = cos_sin_turns(turn)
-    phase = jnp.stack([pc, ps], axis=1)
+    partner = uv_index + 1 - 2 * core
+    m_both = jnp.stack([m_off, partner * width + jnp.arange(width) - G // 2])
 
     fr, fi = factor_table()
-    fr, fi = jnp.asarray(fr.astype(np.float32)), jnp.asarray(fi.astype(np.float32))
-    qt = jnp.mod(jnp.arange(SUB)[:, None] * m_off[None, :], G).astype(jnp.float32) * (1.0 / G)
-    qc, qs = cos_sin_turns(qt)
-    mm = functools.partial(jnp.einsum, "qk,qm->km", precision=lax.Precision.HIGHEST)
-    dr = (mm(fr, qc) - mm(fi, qs)) * (1.0 / SUB)
-    di = (mm(fr, qs) + mm(fi, qc)) * (1.0 / SUB)
+    fr, fi = fr.astype(np.float32), fi.astype(np.float32)
+    qt = jnp.mod(jnp.arange(SUB)[:, None] * m_both.reshape(-1)[None, :], G).astype(jnp.float32)
+    qc, qs = cos_sin_turns(qt * (1.0 / G))
+    both = jnp.dot(
+        jnp.asarray(np.block([[fr.T, -fi.T], [fi.T, fr.T]]) / SUB),
+        jnp.concatenate([qc, qs], axis=0),
+        precision=lax.Precision.HIGHEST,
+    )
+    dr, di = both[:SUB].reshape(SUB, 2, width), both[SUB:].reshape(SUB, 2, width)
     ddr = jnp.concatenate([dr, -di], axis=0)
     ddi = jnp.concatenate([di, dr], axis=0)
     d_table = jnp.concatenate(
-        [jnp.concatenate([ddr, ddi], axis=1), jnp.concatenate([-ddi, ddr], axis=1)], axis=0
-    ).astype(jnp.bfloat16)
-
+        [jnp.stack([ddr, ddi], axis=2), jnp.stack([-ddi, ddr], axis=2)], axis=0
+    ).reshape(4 * SUB, 4 * width).astype(jnp.bfloat16)
+
+    rows = packed.shape[0]
+    half_tiles = G // SUB // 2
+    shape = (2, half_tiles, SUB, width)
     spec = pltpu.PrefetchScalarGridSpec(
         num_scalar_prefetch=2,
         grid=(uv_count,),
         in_specs=[
-            pl.BlockSpec((blocks, 4, k_len), lambda j, *_: (j, 0, 0)),
-            pl.BlockSpec((blocks, 2, width), lambda j, *_: (j, 0, 0)),
+            pl.BlockSpec((1, rows, k_len), lambda j, *_: (j, 0, 0)),
+            pl.BlockSpec((1, blocks, 1), lambda j, *_: (j, 0, 0)),
+            pl.BlockSpec((2, width), lambda j, *_: (0, 0)),
             pl.BlockSpec((2 * SUB, 2 * SUB), lambda j, *_: (0, 0)),
-            pl.BlockSpec((4 * SUB, 2 * width), lambda j, *_: (0, 0)),
+            pl.BlockSpec((4 * SUB, 4 * width), lambda j, *_: (0, 0)),
         ],
-        out_specs=pl.BlockSpec((2, G, width), lambda j, *_: (0, 0, 0)),
-        scratch_shapes=[pltpu.VMEM((2, G, width), jnp.float32)],
-    )
-    half = pl.pallas_call(
-        functools.partial(grid_kernel, width),
-        out_shape=jax.ShapeDtypeStruct((2, G, width), jnp.bfloat16),
+        out_specs=[pl.BlockSpec(shape, lambda j, *_: (0, 0, 0, 0))] * 2,
+        scratch_shapes=[
+            pltpu.VMEM((4, G // 2, width), jnp.float32),
+            pltpu.VMEM((rows, k_len), jnp.float32),
+            pltpu.VMEM((4, blocks, width), jnp.float32),
+            pltpu.SMEM((blocks + UNROLL,), jnp.int32),
+        ],
+    )
+    own, give = pl.pallas_call(
+        functools.partial(grid_kernel, width, blocks),
+        out_shape=[jax.ShapeDtypeStruct(shape, jnp.bfloat16)] * 2,
         grid_spec=spec,
         compiler_params=pltpu.CompilerParams(vmem_limit_bytes=40 * 1024 * 1024),
-    )(tiles, counts, all_data, phase, jnp.asarray(factor_matrix()), d_table)
+    )(tiles, counts, all_data, cols, m_both, jnp.asarray(factor_matrix()), d_table)
+    came_half = lax.ppermute(give, "uv", [(n, n ^ 1) for n in range(uv_count)])
+    half = jnp.concatenate([own, came_half], axis=0)
 
     first = jnp.dot(
-        jnp.asarray(head_matrix()),
+        jnp.asarray(head_matrices())[core],
         half.reshape(2 * 64, 64 * width),
         preferred_element_type=jnp.float32,
     ).astype(jnp.bfloat16)

time: 275 us -> 166 us (0.60)
  blocking collectives: 63.2 us -> 0 us
  between operations: 15 us -> 0.98 us
  Pallas kernels: 117 us -> 104 us
  local copies, waits for them, and re-layouts: 30.7 us -> 19 us
  other arithmetic: 20.4 us -> 10.6 us
  waiting for transfers between devices: 17 us -> 24.7 us
  matrix products: 10.8 us -> 5.19 us
  starting transfers between devices: 0.58 us -> 3.61 us
    unnamed x1 -> x0, blocking collectives: 63.2 us -> none
    pallas_call x1 -> x2, Pallas kernels: 117 us -> 104 us  [the longest x1 82.9 us: on_device(): pl.pallas_call(functools.partial(grid_kernel, width, blocks), out_shape=[...]
    reshape x2 -> x1, local copies, waits for them, and re-layouts: 7.48 us -> 0.01 us  [on_device(): both[:SUB].reshape(SUB, 2, width)]
    add x1, other arithmetic: 7.25 us -> 0.04 us  [on_device(): cols = (came_numbers[:, 1] * SUB + came_numbers[:, 2])[:, :, None]]
    convert_element_type x1, local copies, waits for them, and re-layouts: 6.36 us -> 0.37 us  [on_device(): d_table = jnp.concatenate([jnp.stack([ddr, ddi], axis=2), jnp.stack([-ddi...]
    dot_general x5 -> x3, matrix products: 9.61 us -> 3.95 us  [the longest x2 2.71 us: on_device(): jnp.dot(jnp.asarray(np.block([[fr.T, -fi.T], [fi.T, fr.T]]) / SUB), jnp.c...]
    ppermute x0 -> x1, waiting for transfers between devices: none -> 4.34 us  [on_device(): came_half = lax.ppermute(give, 'uv', [(n, n ^ 1) for n in range(uv_count)])]
    ppermute x1, waiting for transfers between devices: 17 us -> 20.4 us  [on_device(): lax.ppermute(there.transpose(1, 2, 0).reshape(width, -1).astype(jnp.bfloa...]
  transfers between devices with their start and end apart: 2 -> 2, of which waited for: 1 -> 2; matrix products, arithmetic and copies ran while one was open for 7% -> 2% of each run, Pallas kernels for 0% -> 0%
where the time goes in v1:
time: 166 us; the launch traced here: 168 us
  Pallas kernels  104 us (63%)
  waiting for transfers between devices  24.7 us (15%)
  local copies, waits for them, and re-layouts  19 us (11%)
  other arithmetic  10.6 us (6%)
  matrix products  5.19 us (3%)
  starting transfers between devices  3.61 us (2%)
    pallas_call x1, Pallas kernels, on_device(): pl.pallas_call(functools.partial(grid_kernel, width, blocks), out_shape=[...  82.9 us
    pallas_call x1, Pallas kernels, gather_all(): pl.pallas_call(functools.partial(gather_kernel, far, near), out_shape=jax...  20.8 us
    ppermute x1, waiting for transfers between devices, on_device(): lax.ppermute(there.transpose(1, 2, 0).reshape(width, -1).astype(jnp.bfloa...  20.4 us
    unnamed x17, local copies, waits for them, and re-layouts  8.42 us
    mul x1, other arithmetic, on_device(): screened = (image[:, :, :64] * sc - image[:, :, 64:] * ss) * (1.0 / G)  6.78 us
    ppermute x1, waiting for transfers between devices, on_device(): came_half = lax.ppermute(give, 'uv', [(n, n ^ 1) for n in range(uv_count)])  4.34 us
    ppermute x1, starting transfers between devices, on_device(): lax.ppermute(there.transpose(1, 2, 0).reshape(width, -1).astype(jnp.bfloa...  3.6 us
  transfers between devices with their start and end apart: 2, of which 2 were waited for; matrix products, arithmetic and copies ran while one was open for 2% of the time, Pallas kernels for 0%

profile of v1, /device:TPU:0, one launch (start us, length us, event | category | flops | bytes accessed | tf_op | source)
XLA Modules:
  0.0 167.8 jit_solution(7799405034654412795)
XLA Ops:
  0.0 1.4 fusion.38
  1.4 1.4 fusion.10
  2.8 1.0 fusion.99
  3.8 0.0 copy-start.1
  3.8 1.0 fusion.98
  4.8 0.7 convert_bitcast_fusion
  6.1 0.7 convert_bitcast_fusion.1
  6.8 0.1 pad.25.clone
  6.9 0.1 maximum_maximum_fusion.1
  6.9 20.8 %shard_map.91.data_ref = bf16[16,208,256]{2,1,0:T(8,128)(2,1)S(1)} custom-call(bf16[208,256]{1,0:T(8,128)(2,1)S(1)} %constant_dynamic-update-slice_fusion.x_ref), custom_call_target="tpu_custom_call" | custom-call | tf_op jit(solution)/shard_map/pallas_call | solution.py:163
  27.7 0.4 slice_reduce_fusion
  28.2 0.1 concatenate.41
  28.3 0.1 concatenate.42
  28.5 0.5 copy.28
  29.1 0.4 convert_element_type.46.d_ref
  29.5 0.2 copy.29.cols_ref
  29.7 0.1 reshape_squeeze.3.tiles
  29.7 0.1 pad_add_fusion.1.counts
  29.8 0.0 copy-done.1
  29.8 82.9 %shard_map.92 = (bf16[2,32,64,256]{3,2,1,0:T(8,128)(2,1)S(1)}, bf16[2,32,64,256]{3,2,1,0:T(8,128)(2,1)}) custom-call(s32[768]{0:T(1024)S(1)} %reshape_squeeze.3.tiles, s32[17]{0:T(128)S(1)} %pad_add_fusion.1.counts, bf16[16,208,256]{2,1,0:T(8,128)(2,1)S(1)} %shard_map.91.data_ref, s32[16,48,1]{2,1,0:T(8,128)S(1)} %copy.29.cols_ref, ...), custom_call_target="tpu_custom_call" | custom-call | tf_op jit(solution)/shard_map/pallas_call | solution.py:332
  112.7 0.0 copy-start
  112.7 1.3 copy-done
  114.1 0.0 collective-permute-start
  114.1 4.3 %collective-permute-done = bf16[2,32,64,256]{3,2,1,0:T(8,128)(2,1)S(1)} collective-permute-done((bf16[2,32,64,256]{3,2,1,0:T(8,128)(2,1)}, bf16[2,32,64,256]{3,2,1,0:T(8,128)(2,1)S(1)}, u32[]{:S(2)}, u32[]{:S(2)}) %collective-permute-start) | collective-permute-done | bytes 2097184 | tf_op jit(solution)/shard_map/ppermute | solution.py:338
  118.4 2.0 %pad_maximum_fusion = bf16[4,32,64,256]{3,2,1,0:T(8,128)(2,1)S(1)} fusion(bf16[2,32,64,256]{3,2,1,0:T(8,128)(2,1)S(1)} %collective-permute-done, bf16[2,32,64,256]{3,2,1,0:T(8,128)(2,1)} %copy-done), kind=kLoop, calls=%fused_computation.7 | loop fusion | flops 2097152 | bytes 8388608 | tf_op jit(solution)/shard_map/concatenate | solution.py:339
  120.4 0.0 copy-start.4
  120.4 2.9 %copy.42 = bf16[16,8,64,256]{3,1,2,0:T(8,128)(2,1)S(1)} copy(bf16[16,8,64,256]{3,2,1,0:T(8,128)(2,1)S(1)} %bitcast.79) | data formatting | bytes 8388608
  123.3 0.0 copy-done.4
  123.3 1.2 convolution_convert_fusion
  124.5 1.2 copy.43
  125.8 0.6 bitcast_bitcast_fusion
  126.3 0.0 copy-start.3
  126.4 0.6 copy.30
  126.9 1.0 copy-done.3
  127.9 1.2 fusion.100
  129.2 6.8 %fusion.1 = f32[64,256,64]{1,2,0:T(8,128)S(1)} fusion(f32[64,256,128]{1,2,0:T(8,128)S(1)} %fusion.100, f32[64,64]{1,0:T(8,128)S(1)} %multiply_multiply_fusion.16, f32[256]{0:T(256)S(1)} %multiply_subtract_fusion, f32[]{:T(128)S(6)} %mul.191), kind=kLoop, calls=%fused_computation.5 | loop fusion | flops 40894464 | bytes 12600324 | tf_op jit(solution)/shard_map/mul | solution.py:356
  136.0 0.0 copy-start.2
  136.0 1.9 %copy-done.2 = f32[64,256,64]{1,2,0:T(8,128)} copy-done((f32[64,256,64]{1,2,0:T(8,128)}, f32[64,256,64]{1,2,0:T(8,128)S(1)}, u32[]{:S(2)}) %copy-start.2) | copy-done | bytes 4194328
  137.9 0.2 fusion.11
  138.1 0.6 copy.32
  138.7 3.6 %collective-permute-start.1 = (bf16[256,2048]{0,1:T(8,128)(2,1)S(1)}, bf16[256,2048]{0,1:T(8,128)(2,1)S(1)}, u32[]{:S(2)}, u32[]{:S(2)}) collective-permute-start(bf16[256,2048]{0,1:T(8,128)(2,1)S(1)} %bitcast.82), channel_id=1, source_target_pairs={{0,16},{16,0},{1,17},{17,1},{2,18},{18,2},{3,19},{19,3},{4,20},{20... | collective-permute-start | bytes 3145736 | tf_op jit(solution)/shard_map/ppermute | solution.py:361
  142.3 1.8 %dynamic-slice_bitcast_fusion = f32[256,32,64]{0,1,2:T(8,128)S(1)} fusion(f32[64,256,64]{1,2,0:T(8,128)} %copy-done.2, s32[]{:T(128)S(6)} %select_n.38), kind=kLoop, calls=%fused_computation.26 | loop fusion | bytes 4194308 | tf_op jit(solution)/shard_map/transpose | solution.py:366
  144.1 1.2 copy.31
  145.4 20.4 %collective-permute-done.1 = bf16[256,2048]{0,1:T(8,128)(2,1)S(1)} collective-permute-done((bf16[256,2048]{0,1:T(8,128)(2,1)S(1)}, bf16[256,2048]{0,1:T(8,128)(2,1)S(1)}, u32[]{:S(2)}, u32[]{:S(2)}) %collective-permute-start.1) | collective-permute-done | bytes 1048608 | tf_op jit(solution)/shard_map/ppermute | solution.py:361
  165.7 0.2 bitcast_add_fusion
  166.0 1.8 %copy.33 = f32[256,2048]{1,0:T(8,128)} copy(f32[256,2048]{0,1:T(8,128)S(1)} %bitcast_add_fusion) | data formatting | bytes 4194304 | tf_op jit(solution)/shard_map/add | solution.py:366
  (24 shorter events, 0.3 us)
Async XLA Ops:
  3.8 26.1 %copy-start.1 = (bf16[128,128]{1,0:T(8,128)(2,1)S(1)}, bf16[128,128]{1,0:T(8,128)(2,1)}, u32[]{:S(2)}) copy-start(bf16[128,128]{1,0:T(8,128)(2,1)} %constant.150.clone.mf_ref) | copy-start | bytes 98308
  112.7 1.3 copy-start
  114.1 4.4 %collective-permute-start = (bf16[2,32,64,256]{3,2,1,0:T(8,128)(2,1)}, bf16[2,32,64,256]{3,2,1,0:T(8,128)(2,1)S(1)}, u32[]{:S(2)}, u32[]{:S(2)}) collective-permute-start(bf16[2,32,64,256]{3,2,1,0:T(8,128)(2,1)} %get-tuple-element.8), channel_id=1, source_target_pairs={{0,1},{1,0},{2,3},{3,2},{4,5},{5,4},{6,7},{7,6},{8,9},{9,8},{10,11... | collective-permute-start | bytes 6291464 | tf_op jit(solution)/shard_map/ppermute | solution.py:338
  120.4 2.9 %copy-start.4 = (bf16[2,128,128]{2,1,0:T(8,128)(2,1)S(1)}, bf16[2,128,128]{2,1,0:T(8,128)(2,1)}, u32[]{:S(2)}) copy-start(bf16[2,128,128]{2,1,0:T(8,128)(2,1)} %constant.151.clone) | copy-start | bytes 196612
  126.3 1.6 copy-start.3
  136.0 1.9 %copy-start.2 = (f32[64,256,64]{1,2,0:T(8,128)}, f32[64,256,64]{1,2,0:T(8,128)S(1)}, u32[]{:S(2)}) copy-start(f32[64,256,64]{1,2,0:T(8,128)S(1)} %fusion.1) | copy-start | bytes 12582916
  138.7 27.1 %collective-permute-start.1 = (bf16[256,2048]{0,1:T(8,128)(2,1)S(1)}, bf16[256,2048]{0,1:T(8,128)(2,1)S(1)}, u32[]{:S(2)}, u32[]{:S(2)}) collective-permute-start(bf16[256,2048]{0,1:T(8,128)(2,1)S(1)} %bitcast.82), channel_id=1, source_target_pairs={{0,16},{16,0},{1,17},{17,1},{2,18},{18,2},{3,19},{19,3},{4,20},{20... | collective-permute-start | bytes 3145736 | tf_op jit(solution)/shard_map/ppermute | solution.py:361

commit v2 on v1

--- a/solution.py
+++ b/solution.py
@@ -12,7 +12,7 @@
 
 G = 4096
 SUB = 64
-UNROLL = 4
+UNROLL = 8
 plane_step = 6.0
 full_turn = 2.0 * math.pi
 BF = ml_dtypes.bfloat16
@@ -88,6 +88,11 @@
     top = np.concatenate([c, s], axis=2)
     bottom = np.concatenate([-s, c], axis=2)
     return np.concatenate([top, bottom], axis=1).astype(BF)
+
+
+def split_tail(parts):
+    whole = tail_matrices().reshape(64, 128, 2, parts, 64 // parts)
+    return np.ascontiguousarray(whole.transpose(3, 0, 1, 2, 4)).reshape(parts, 64, 128, -1)
 
 
 def gather_kernel(far, near, x_ref, out_ref, z_send, z_recv, y_send, y_recv, c_send, c_recv):
@@ -176,26 +181,25 @@
     width, blocks, tiles, counts, data_ref, cols_ref, moff_ref, mf_ref, d_ref,
     keep_ref, give_ref, acc, rows_f, phase, mine,
 ):
-    j = pl.program_id(0)
-    steps = pl.num_programs(0)
-
-    @pl.when(j == 0)
-    def _():
-        acc[...] = jnp.zeros_like(acc)
-
-    core = counts[steps]
-    rows_f[...] = data_ref[0].astype(jnp.float32)
-    for h in range(2):
-        turn = jnp.bitwise_and((cols_ref[0] - G // 2) * moff_ref[h : h + 1, :], G - 1)
-        pc, ps = cos_sin_turns(turn.astype(jnp.float32) * (1.0 / G))
-        phase[2 * h] = pc
-        phase[2 * h + 1] = ps
-
-    def pick(i, n):
-        mine[n] = i
-        return n + jnp.where(lax.rem(tiles[j * blocks + i], 2) == core, 1, 0)
-
-    total = lax.fori_loop(0, counts[j], pick, 0)
+    devices = data_ref.shape[0]
+    acc[...] = jnp.zeros_like(acc)
+    core = counts[devices]
+
+    def spread(j, found):
+        rows_f[j] = data_ref[j].astype(jnp.float32)
+        for h in range(2):
+            turn = jnp.bitwise_and((cols_ref[j] - G // 2) * moff_ref[h : h + 1, :], G - 1)
+            pc, ps = cos_sin_turns(turn.astype(jnp.float32) * (1.0 / G))
+            phase[j, 2 * h] = pc
+            phase[j, 2 * h + 1] = ps
+
+        def pick(i, n):
+            mine[n] = j * blocks + i
+            return n + jnp.where(lax.rem(tiles[j * blocks + i], 2) == core, 1, 0)
+
+        return lax.fori_loop(0, counts[j], pick, found)
+
+    total = lax.fori_loop(0, devices, spread, 0)
     k_len = data_ref.shape[2]
     offs = lax.broadcasted_iota(jnp.int32, (8, k_len), 0).astype(jnp.float32)
     fine = offs * (1.0 / SUB)
@@ -214,10 +218,12 @@
         lefts, rights, index = [], [], []
         for k in range(UNROLL):
             n = it * UNROLL + k
-            i = jnp.where(n < total, mine[n], 0)
-            index.append(i)
+            g = jnp.where(n < total, mine[n], 0)
+            j = g // blocks
+            i = g - j * blocks
+            index.append((g, j, i))
             keep = jnp.where(n < total, scale, 0.0)
-            vr, vi, u, v = (rows_f[pl.ds(q * blocks + i, 1), :] for q in range(4))
+            vr, vi, u, v = (rows_f[j, pl.ds(q * blocks + i, 1), :] for q in range(4))
             c1, s1 = cos_sin_turns(fine * u)
             c8, s8 = cos_sin_turns(coarse * u)
             lefts.append(
@@ -241,24 +247,22 @@
                 preferred_element_type=jnp.float32,
             )
             for k in range(UNROLL):
-                i = index[k]
-                pr = phase[2 * h, pl.ds(i, 1), :]
-                pi = phase[2 * h + 1, pl.ds(i, 1), :]
+                g, j, i = index[k]
+                pr = phase[j, 2 * h, pl.ds(i, 1), :]
+                pi = phase[j, 2 * h + 1, pl.ds(i, 1), :]
                 hr = out[k * SUB : (k + 1) * SUB, :width]
                 hi = out[k * SUB : (k + 1) * SUB, width:]
-                rows = pl.ds(pl.multiple_of(tiles[j * blocks + i] // 2 * SUB, SUB), SUB)
+                rows = pl.ds(pl.multiple_of(tiles[g] // 2 * SUB, SUB), SUB)
                 acc[2 * h, rows, :] += hr * pr - hi * pi
                 acc[2 * h + 1, rows, :] += hr * pi + hi * pr
         return carry
 
     lax.fori_loop(0, (total + UNROLL - 1) // UNROLL, step, 0)
 
-    @pl.when(j == steps - 1)
-    def _():
-        half_rows = acc.shape[1] // SUB
-        for h, ref in enumerate((keep_ref, give_ref)):
-            for c in range(2):
-                ref[c] = acc[2 * h + c].astype(jnp.bfloat16).reshape(half_rows, SUB, width)
+    half_rows = acc.shape[1] // SUB
+    for h, ref in enumerate((keep_ref, give_ref)):
+        for c in range(2):
+            ref[c] = acc[2 * h + c].astype(jnp.bfloat16).reshape(half_rows, SUB, width)
 
 
 def on_device(visibility, coords, tile_row, col_offset, live_count):
@@ -311,29 +315,20 @@
     rows = packed.shape[0]
     half_tiles = G // SUB // 2
     shape = (2, half_tiles, SUB, width)
-    spec = pltpu.PrefetchScalarGridSpec(
-        num_scalar_prefetch=2,
-        grid=(uv_count,),
-        in_specs=[
-            pl.BlockSpec((1, rows, k_len), lambda j, *_: (j, 0, 0)),
-            pl.BlockSpec((1, blocks, 1), lambda j, *_: (j, 0, 0)),
-            pl.BlockSpec((2, width), lambda j, *_: (0, 0)),
-            pl.BlockSpec((2 * SUB, 2 * SUB), lambda j, *_: (0, 0)),
-            pl.BlockSpec((4 * SUB, 4 * width), lambda j, *_: (0, 0)),
-        ],
-        out_specs=[pl.BlockSpec(shape, lambda j, *_: (0, 0, 0, 0))] * 2,
-        scratch_shapes=[
-            pltpu.VMEM((4, G // 2, width), jnp.float32),
-            pltpu.VMEM((rows, k_len), jnp.float32),
-            pltpu.VMEM((4, blocks, width), jnp.float32),
-            pltpu.SMEM((blocks + UNROLL,), jnp.int32),
-        ],
-    )
+    vmem = pl.BlockSpec(memory_space=pltpu.VMEM)
+    smem = pl.BlockSpec(memory_space=pltpu.SMEM)
     own, give = pl.pallas_call(
         functools.partial(grid_kernel, width, blocks),
         out_shape=[jax.ShapeDtypeStruct(shape, jnp.bfloat16)] * 2,
-        grid_spec=spec,
-        compiler_params=pltpu.CompilerParams(vmem_limit_bytes=40 * 1024 * 1024),
+        in_specs=[smem, smem, vmem, vmem, vmem, vmem, vmem],
+        out_specs=[vmem, vmem],
+        scratch_shapes=[
+            pltpu.VMEM((4, G // 2, width), jnp.float32),
+            pltpu.VMEM((uv_count, rows, k_len), jnp.float32),
+            pltpu.VMEM((uv_count, 4, blocks, width), jnp.float32),
+            pltpu.SMEM((uv_count * blocks + UNROLL,), jnp.int32),
+        ],
+        compiler_params=pltpu.CompilerParams(vmem_limit_bytes=48 * 1024 * 1024),
     )(tiles, counts, all_data, cols, m_both, jnp.asarray(factor_matrix()), d_table)
     came_half = lax.ppermute(give, "uv", [(n, n ^ 1) for n in range(uv_count)])
     half = jnp.concatenate([own, came_half], axis=0)
@@ -344,28 +339,30 @@
         preferred_element_type=jnp.float32,
     ).astype(jnp.bfloat16)
     first = first.reshape(2, 64, 64, width).transpose(1, 0, 2, 3).reshape(64, 128, width)
-    image = jnp.einsum(
-        "lxm,lxy->lmy", first, jnp.asarray(tail_matrices()), preferred_element_type=jnp.float32
-    )
-    l_of = jnp.arange(64)[:, None, None] + 64 * jnp.arange(64)[None, None, :] - G // 2
-    x = l_of.astype(jnp.float32) / G
+    share = 64 // wa_count
+    depth = (wa_index.astype(jnp.float32) - (wa_count - 1) / 2.0) * plane_step
     y = m_off[None, :, None].astype(jnp.float32) / G
-    depth_term = jnp.sqrt(1.0 - y**2 - x**2)
-    depth = (wa_index.astype(jnp.float32) - (wa_count - 1) / 2.0) * plane_step
-    sc, ss = cos_sin_turns(depth * (depth_term - 1.0))
-    screened = (image[:, :, :64] * sc - image[:, :, 64:] * ss) * (1.0 / G)
-    share = 64 // wa_count
+    tail = jnp.asarray(split_tail(wa_count))
+
+    def shares_of(part):
+        image = jnp.einsum("lxm,lxy->lmy", first, tail[part], preferred_element_type=jnp.float32)
+        l1 = part * share + jnp.arange(share)[None, None, :]
+        x = (jnp.arange(64)[:, None, None] + 64 * l1 - G // 2).astype(jnp.float32) / G
+        depth_term = jnp.sqrt(1.0 - y**2 - x**2)
+        sc, ss = cos_sin_turns(depth * (depth_term - 1.0))
+        screened = (image[:, :, :share] * sc - image[:, :, share:] * ss) * (1.0 / G)
+        return screened
+
+    def in_order(screened):
+        return screened.transpose(1, 2, 0).reshape(width, G // wa_count)
+
     if wa_count == 2:
-        there = lax.dynamic_slice_in_dim(screened, (1 - wa_index) * share, share, 2)
-        here = lax.dynamic_slice_in_dim(screened, wa_index * share, share, 2)
-        came = lax.ppermute(
-            there.transpose(1, 2, 0).reshape(width, -1).astype(jnp.bfloat16),
-            "wa",
-            [(0, 1), (1, 0)],
-        )
-        return here.transpose(1, 2, 0).reshape(width, -1) + came.astype(jnp.float32)
-    parts = screened.transpose(1, 2, 0).reshape(width, G).astype(jnp.bfloat16)
-    parts = parts.reshape(width, wa_count, G // wa_count)
+        away = in_order(shares_of(1 - wa_index).astype(jnp.bfloat16))
+        came = lax.ppermute(away, "wa", [(0, 1), (1, 0)])
+        return in_order(shares_of(wa_index)) + came.astype(jnp.float32)
+    parts = jnp.stack(
+        [in_order(shares_of(part).astype(jnp.bfloat16)) for part in range(wa_count)], axis=1
+    )
     came = lax.all_to_all(parts, "wa", split_axis=1, concat_axis=1)
     return jnp.sum(came.astype(jnp.float32), axis=1)
 

time: 166 us -> 142 us (0.86)
  Pallas kernels: 104 us -> 80 us
  local copies, waits for them, and re-layouts: 19 us -> 13.3 us
  waiting for transfers between devices: 24.7 us -> 28.2 us
  starting transfers between devices: 3.61 us -> 5.43 us
    pallas_call x1, Pallas kernels: 82.9 us -> 59.2 us  [on_device(): pl.pallas_call(functools.partial(grid_kernel, width, blocks), out_shape=[...]
    transpose x0 -> x1, other arithmetic: none -> 6.81 us  [in_order(): return screened.transpose(1, 2, 0).reshape(width, G // wa_count)]
    mul x2, other arithmetic: 6.79 us -> 0.01 us  [shares_of(): 64 * l1]
    ppermute x1, starting transfers between devices: 0.01 us -> 5.36 us  [on_device(): came_half = lax.ppermute(give, 'uv', [(n, n ^ 1) for n in range(uv_count)])]
    ppermute x1, waiting for transfers between devices: 20.4 us -> 24.2 us  [on_device(): came = lax.ppermute(away, 'wa', [(0, 1), (1, 0)])]
    ppermute x1, starting transfers between devices: 3.6 us -> 0.07 us  [on_device(): came = lax.ppermute(away, 'wa', [(0, 1), (1, 0)])]
    unnamed x17 -> x23, local copies, waits for them, and re-layouts: 8.42 us -> 6.49 us
  transfers between devices with their start and end apart: 2 -> 2, of which waited for: 2 -> 2; matrix products, arithmetic and copies ran while one was open for 2% -> 1% of each run, Pallas kernels for 0% -> 0%
where the time goes in v2:
time: 142 us; the launch traced here: 143 us
  Pallas kernels  80 us (56%)
  waiting for transfers between devices  28.2 us (20%)
  local copies, waits for them, and re-layouts  13.3 us (9%)
  other arithmetic  9.33 us (7%)
  starting transfers between devices  5.43 us (4%)
  matrix products  5.42 us (4%)
    pallas_call x1, Pallas kernels, on_device(): pl.pallas_call(functools.partial(grid_kernel, width, blocks), out_shape=[...  59.2 us
    ppermute x1, waiting for transfers between devices, on_device(): came = lax.ppermute(away, 'wa', [(0, 1), (1, 0)])  24.2 us
    pallas_call x1, Pallas kernels, gather_all(): pl.pallas_call(functools.partial(gather_kernel, far, near), out_shape=jax...  20.8 us
    transpose x1, other arithmetic, in_order(): return screened.transpose(1, 2, 0).reshape(width, G // wa_count)  6.81 us
    unnamed x23, local copies, waits for them, and re-layouts  6.49 us
    ppermute x1, starting transfers between devices, on_device(): came_half = lax.ppermute(give, 'uv', [(n, n ^ 1) for n in range(uv_count)])  5.36 us
    ppermute x1, waiting for transfers between devices, on_device(): came_half = lax.ppermute(give, 'uv', [(n, n ^ 1) for n in range(uv_count)])  3.96 us
  transfers between devices with their start and end apart: 2, of which 2 were waited for; matrix products, arithmetic and copies ran while one was open for 1% of the time, Pallas kernels for 0%

profile of v2, /device:TPU:0, one launch (start us, length us, event | category | flops | bytes accessed | tf_op | source)
XLA Modules:
  0.0 142.6 jit_solution(4706232498186942196)
XLA Ops:
  0.0 0.0 copy-start.3
  0.0 0.0 copy-start.4
  0.0 0.0 copy-start.6
  0.0 0.0 copy-start.7
  0.0 1.4 fusion.56
  1.4 1.4 fusion.22
  2.8 0.0 copy-done.3
  2.9 0.1 fusion.119
  2.9 0.0 copy-done.4
  3.0 0.1 fusion.118
  3.0 0.0 copy-done.6
  3.7 0.0 copy-done.7
  3.8 0.1 pad.25.clone
  3.9 0.1 maximum_maximum_fusion.1
  3.9 20.8 %shard_map.91.data_ref = bf16[16,208,256]{2,1,0:T(8,128)(2,1)S(1)} custom-call(bf16[208,256]{1,0:T(8,128)(2,1)S(1)} %constant_dynamic-update-slice_fusion.x_ref), custom_call_target="tpu_custom_call" | custom-call | tf_op jit(solution)/shard_map/pallas_call | solution.py:168
  24.7 0.4 slice_reduce_fusion
  25.2 0.1 concatenate.41
  25.3 0.1 concatenate.42
  25.5 0.0 copy-start.1
  25.6 0.5 copy.28
  26.1 0.4 convert_element_type.48.d_ref
  26.5 0.2 copy.29.cols_ref
  26.7 0.1 reshape_squeeze.3.tiles
  26.8 0.1 pad_add_fusion.1.counts
  26.8 0.0 copy-done.1
  26.8 59.2 %shard_map.92 = (bf16[2,32,64,256]{3,2,1,0:T(8,128)(2,1)S(1)}, bf16[2,32,64,256]{3,2,1,0:T(8,128)(2,1)}) custom-call(s32[768]{0:T(1024)S(1)} %reshape_squeeze.3.tiles, s32[17]{0:T(128)S(1)} %pad_add_fusion.1.counts, bf16[16,208,256]{2,1,0:T(8,128)(2,1)S(1)} %shard_map.91.data_ref, s32[16,48,1]{2,1,0:T(8,128)S(1)} %copy.29.cols_ref, ...), custom_call_target="tpu_custom_call" | custom-call | tf_op jit(solution)/shard_map/pallas_call | solution.py:320
  86.0 1.3 copy-done
  87.4 5.4 %collective-permute-start = (bf16[2,32,64,256]{3,2,1,0:T(8,128)(2,1)}, bf16[2,32,64,256]{3,2,1,0:T(8,128)(2,1)S(1)}, u32[]{:S(2)}, u32[]{:S(2)}) collective-permute-start(bf16[2,32,64,256]{3,2,1,0:T(8,128)(2,1)} %get-tuple-element.8), channel_id=1, source_target_pairs={{0,1},{1,0},{2,3},{3,2},{4,5},{5,4},{6,7},{7,6},{8,9},{9,8},{10,11... | collective-permute-start | bytes 6291464 | tf_op jit(solution)/shard_map/ppermute | solution.py:333
  92.8 4.0 %collective-permute-done = bf16[2,32,64,256]{3,2,1,0:T(8,128)(2,1)S(1)} collective-permute-done((bf16[2,32,64,256]{3,2,1,0:T(8,128)(2,1)}, bf16[2,32,64,256]{3,2,1,0:T(8,128)(2,1)S(1)}, u32[]{:S(2)}, u32[]{:S(2)}) %collective-permute-start) | collective-permute-done | bytes 2097184 | tf_op jit(solution)/shard_map/ppermute | solution.py:333
  96.7 2.0 %pad_maximum_fusion = bf16[4,32,64,256]{3,2,1,0:T(8,128)(2,1)S(1)} fusion(bf16[2,32,64,256]{3,2,1,0:T(8,128)(2,1)S(1)} %collective-permute-done, bf16[2,32,64,256]{3,2,1,0:T(8,128)(2,1)} %copy-done), kind=kLoop, calls=%fused_computation.2 | loop fusion | flops 2097152 | bytes 8388608 | tf_op jit(solution)/shard_map/concatenate | solution.py:334
  98.7 0.0 copy-start.5
  98.7 2.9 %copy.42 = bf16[16,8,64,256]{3,1,2,0:T(8,128)(2,1)S(1)} copy(bf16[16,8,64,256]{3,2,1,0:T(8,128)(2,1)S(1)} %bitcast.86) | data formatting | bytes 8388608
  101.6 0.0 copy-done.5
  101.6 1.2 convolution_convert_fusion
  102.8 1.2 copy.43
  104.1 0.6 bitcast_bitcast_fusion
  104.7 0.0 copy-start.2
  104.7 0.6 copy.30
  105.2 1.0 copy-done.2
  106.2 0.7 fusion.25
  107.0 0.7 fusion.23
  107.7 6.8 %fusion.29 = (bf16[256,32,64]{0,1,2:T(8,128)(2,1)S(1)}, f32[256,32,64]{0,1,2:T(8,128)S(1)}) fusion(f32[64,256,64]{1,2,0:T(8,128)S(1)} %fusion.23, f32[64,32]{1,0:T(8,128)S(1)} %get-tuple-element.29, f32[256]{0:T(256)S(1)} %multiply_subtract_fusion, f32[]{:T(128)S(6)} %mul.248, f32[64,256,64]{1,2,0:T(8,128)S(1)} %fusion.25, f32[64,32]{1,0:T(8,128)S(1)} %get-tuple-element.30), kind=kLoop, calls=%fused_computation.56 | loop fusion | flops 41418752 | bytes 11551748 | tf_op jit(solution)/shard_map/transpose | solution.py:357
  114.5 0.6 copy.32
  115.1 0.1 collective-permute-start.1
  115.2 1.2 copy.31
  116.4 24.2 %collective-permute-done.1 = bf16[256,2048]{0,1:T(8,128)(2,1)S(1)} collective-permute-done((bf16[256,2048]{0,1:T(8,128)(2,1)S(1)}, bf16[256,2048]{0,1:T(8,128)(2,1)S(1)}, u32[]{:S(2)}, u32[]{:S(2)}) %collective-permute-start.1) | collective-permute-done | bytes 1048608 | tf_op jit(solution)/shard_map/ppermute | solution.py:361
  140.6 0.2 bitcast_add_fusion
  140.8 1.8 %copy.33 = f32[256,2048]{1,0:T(8,128)} copy(f32[256,2048]{0,1:T(8,128)S(1)} %bitcast_add_fusion) | data formatting | bytes 4194304 | tf_op jit(solution)/shard_map/add | solution.py:362
  (28 shorter events, 0.3 us)
Async XLA Ops:
  0.0 2.8 %copy-start.3 = (bf16[48,2,256]{2,1,0:T(2,128)(2,1)S(1)}, bf16[48,2,256]{2,1,0:T(2,128)(2,1)}, u32[]{:S(2)}) copy-start(bf16[48,2,256]{2,1,0:T(2,128)(2,1)} %param.9) | copy-start | bytes 147460
  0.0 2.9 %copy-start.4 = (bf16[48,2,256]{2,1,0:T(2,128)(2,1)S(1)}, bf16[48,2,256]{2,1,0:T(2,128)(2,1)}, u32[]{:S(2)}) copy-start(bf16[48,2,256]{2,1,0:T(2,128)(2,1)} %param.10) | copy-start | bytes 147460
  0.0 3.0 %copy-start.6 = (s32[48]{0:T(128)S(1)}, s32[48]{0:T(128)}, u32[]{:S(2)}) copy-start(s32[48]{0:T(128)} %param.12) | copy-start | bytes 580
  0.0 3.7 %copy-start.7 = (s32[48,1]{0,1:T(1,128)S(1)}, s32[48,1]{0,1:T(1,128)}, u32[]{:S(2)}) copy-start(s32[48,1]{0,1:T(1,128)} %param.11) | copy-start | bytes 580
  25.5 1.4 copy-start.1
  86.0 1.3 copy-start
  87.4 9.4 %collective-permute-start = (bf16[2,32,64,256]{3,2,1,0:T(8,128)(2,1)}, bf16[2,32,64,256]{3,2,1,0:T(8,128)(2,1)S(1)}, u32[]{:S(2)}, u32[]{:S(2)}) collective-permute-start(bf16[2,32,64,256]{3,2,1,0:T(8,128)(2,1)} %get-tuple-element.8), channel_id=1, source_target_pairs={{0,1},{1,0},{2,3},{3,2},{4,5},{5,4},{6,7},{7,6},{8,9},{9,8},{10,11... | collective-permute-start | bytes 6291464 | tf_op jit(solution)/shard_map/ppermute | solution.py:333
  98.7 2.9 %copy-start.5 = (bf16[2,128,128]{2,1,0:T(8,128)(2,1)S(1)}, bf16[2,128,128]{2,1,0:T(8,128)(2,1)}, u32[]{:S(2)}) copy-start(bf16[2,128,128]{2,1,0:T(8,128)(2,1)} %constant.156.clone) | copy-start | bytes 196612
  104.7 1.6 %copy-start.2 = (bf16[2,64,128,64]{2,3,1,0:T(8,128)(2,1)S(1)}, bf16[2,64,128,64]{2,3,1,0:T(8,128)(2,1)}, u32[]{:S(2)}) copy-start(bf16[2,64,128,64]{2,3,1,0:T(8,128)(2,1)} %constant.157.clone) | copy-start | bytes 6291460
  115.1 25.5 %collective-permute-start.1 = (bf16[256,2048]{0,1:T(8,128)(2,1)S(1)}, bf16[256,2048]{0,1:T(8,128)(2,1)S(1)}, u32[]{:S(2)}, u32[]{:S(2)}) collective-permute-start(bf16[256,2048]{0,1:T(8,128)(2,1)S(1)} %bitcast.89), channel_id=1, source_target_pairs={{0,16},{16,0},{1,17},{17,1},{2,18},{18,2},{3,19},{19,3},{4,20},{20... | collective-permute-start | bytes 3145736 | tf_op jit(solution)/shard_map/ppermute | solution.py:361
